TPU v7x, 32 devices: a whole 2x2x4 slice. The times are simulated.
32 devices in a mesh: ctx: 32 (over z, y, x, core), head: 1.
Axes of the slice: x: 2, y: 2, z: 4, core: 2. Of those that a mesh axis runs over, the one named last changes fastest.
Arguments:
- query_rows: bfloat16 [8192, 1024], P('ctx', 'head'), may hold values from -6 to 6
- key_rows: bfloat16 [8192, 1024], P('ctx', 'head')
- value_rows: bfloat16 [8192, 1024], P('ctx', 'head'), may hold values from -6 to 6
- beta: float32 [8192, 8], P('ctx', 'head'), may hold values from 0 to 2
- norm_gain: float32 [128], replicated, may hold values from 0.1 to 1.9
- out_cotangent: bfloat16 [8192, 4096], P('ctx', 'head'), may hold values from -0.125 to 0.125
Outputs:
- attended: bfloat16 [8192, 1024], P('ctx', 'head')
- weight_grad: float32 [4096, 1024], P('ctx', 'head')
All inputs are finite; a program needn't handle non-finite values.
Results may differ from a plain program's by a relative error of at most 0.0029.
Values may be sent and summed in bfloat16 or wider, within the bound.
A program may use at most 128 MiB of HBM per device.

v0:
```python
import jax
import jax.numpy as jnp
from jax import lax
from jax.sharding import PartitionSpec as P

FEATURE_WIDTHS = 128
GROUP = 64


epsilon = 1e-06
highest = lax.Precision.HIGHEST


def entering(part, axis, combine, identity):
    place = lax.axis_index(axis)
    gathered = jax.tree.map(lambda a: lax.all_gather(a, axis), part)
    state = jax.tree.map(lambda a, e: jnp.zeros_like(a) + jnp.asarray(e, a.dtype), part, identity)

    def one(hop, state):
        return combine(
            state, jax.tree.map(lambda a: lax.dynamic_index_in_dim(a, hop, 0, False), gathered)
        )

    return lax.fori_loop(0, place, one, state)


def matmul(pattern, former, latter):
    return jnp.einsum(
        pattern, former, latter, precision=highest, preferred_element_type=jnp.float32
    )


def unit_lower_inverse(strict_lower):
    negated = -strict_lower
    inverse = jnp.eye(GROUP, dtype=jnp.float32) + negated
    power = negated
    doubling = 2
    while doubling < GROUP:
        power = matmul("...ij,...jk->...ik", power, power)
        inverse = matmul("...ij,...jk->...ik", inverse, jnp.eye(GROUP, dtype=jnp.float32) + power)
        doubling = doubling * 2
    return inverse


def split_heads(array, groups, heads):
    return (
        array.astype(jnp.float32)
        .reshape(groups, GROUP, heads, FEATURE_WIDTHS)
        .transpose(2, 0, 1, 3)
    )


def group_parts(query_rows, key_rows, value_rows, beta, heads, groups):
    query_f = split_heads(query_rows, groups, heads)
    key_raw = split_heads(key_rows, groups, heads)
    key_unit = key_raw * lax.rsqrt(jnp.sum(key_raw * key_raw, axis=-1, keepdims=True) + epsilon)
    value_f = split_heads(value_rows, groups, heads)
    strength = beta.reshape(groups, GROUP, heads).transpose(2, 0, 1)[..., None]
    lower_mask = jnp.tril(jnp.ones((GROUP, GROUP), jnp.float32), -1)
    causal_mask = jnp.tril(jnp.ones((GROUP, GROUP), jnp.float32))
    inverse = unit_lower_inverse(
        lower_mask * (strength * matmul("hnid,hnjd->hnij", key_unit, key_unit))
    )
    stacked = jnp.concatenate([strength * key_unit, strength * value_f], axis=-1)
    solved = matmul("hnij,hnjd->hnid", inverse, stacked)
    scores = causal_mask * matmul("hnid,hnjd->hnij", query_f, key_unit)
    return (query_f, key_unit, solved[..., :FEATURE_WIDTHS], solved[..., FEATURE_WIDTHS:], scores)


def sequence_prefix(dev_trans, dev_state, zeros_state, identity):

    def compose_pairs(earlier, later):
        return (
            matmul("hde,hef->hdf", later[0], earlier[0]),
            matmul("hde,hef->hdf", later[0], earlier[1]) + later[1],
        )

    prefix = entering((dev_trans, dev_state), "ctx", compose_pairs, (identity, zeros_state))
    start_state = prefix[1]
    return start_state


def on_device(query_rows, key_rows, value_rows, beta, norm_gain, out_cotangent):
    tok_rows = query_rows.shape[0]
    heads = beta.shape[1]
    groups = tok_rows // GROUP
    query_f, key_unit, key_mix, value_mix, scores = group_parts(
        query_rows, key_rows, value_rows, beta, heads, groups
    )
    identity = jnp.broadcast_to(
        jnp.eye(FEATURE_WIDTHS, dtype=jnp.float32), (heads, FEATURE_WIDTHS, FEATURE_WIDTHS)
    )
    zeros_state = jnp.zeros((heads, FEATURE_WIDTHS, FEATURE_WIDTHS), jnp.float32)
    transits = jnp.moveaxis(identity[:, None] - matmul("hncd,hnce->hnde", key_unit, key_mix), 1, 0)
    writes = jnp.moveaxis(matmul("hncd,hnce->hnde", key_unit, value_mix), 1, 0)
    query_eff = query_f - matmul("hnij,hnjd->hnid", scores, key_mix)
    local_out = matmul("hnij,hnjd->hnid", scores, value_mix)

    def compose_step(carry, pair):
        product, state = carry
        transit, write = pair
        return (
            matmul("hde,hef->hdf", transit, product),
            matmul("hde,hef->hdf", transit, state) + write,
        )

    def record_step(carry, pair):
        return (compose_step(carry, pair), carry)

    device_pair, history = lax.scan(record_step, (identity, zeros_state), (transits, writes))
    prior_trans = jnp.moveaxis(history[0], 0, 1)
    prior_state = jnp.moveaxis(history[1], 0, 1)
    base_out = local_out + matmul("hncd,hnde->hnce", query_eff, prior_state)
    carried = matmul("hncd,hnde->hnce", query_eff, prior_trans)
    start_state = sequence_prefix(device_pair[0], device_pair[1], zeros_state, identity)
    mixed = base_out + matmul("hncd,hde->hnce", carried, start_state)
    mean_square = jnp.mean(mixed * mixed, axis=-1, keepdims=True)
    normed = mixed * lax.rsqrt(mean_square + epsilon) * norm_gain
    attended = (
        normed.astype(jnp.bfloat16).transpose(1, 2, 0, 3).reshape(tok_rows, heads * FEATURE_WIDTHS)
    )
    full_cotangent = lax.all_gather(out_cotangent, "head", axis=1, tiled=True)
    weight_grad = lax.psum_scatter(
        lax.dot_general(
            full_cotangent, attended, (((0,), (0,)), ((), ())), preferred_element_type=jnp.float32
        ),
        "ctx",
        scatter_dimension=0,
        tiled=True,
    )
    return (attended, weight_grad)


def solution(mesh):
    in_specs = (
        P("ctx", "head"),
        P("ctx", "head"),
        P("ctx", "head"),
        P("ctx", "head"),
        P(),
        P("ctx", "head"),
    )
    out_specs = (P("ctx", "head"), P("ctx", "head"))
    return jax.shard_map(
        on_device, mesh=mesh, in_specs=in_specs, out_specs=out_specs, check_vma=False
    )
```

profile of v0, /device:TPU:0, one launch (start us, length us, event | category | flops | bytes accessed | tf_op | source)
XLA Modules:
  0.0 573.2 jit_solution(12221171184192703908)
XLA Ops:
  10.0 2.2 fusion.26
  20.7 1.5 convolution_add_fusion.3
  25.5 1.9 fusion.14
  27.5 5.1 convolution_bitcast_fusion.1
  32.6 14.5 %subtract_bitcast_fusion = f32[4,8,128,128]{3,2,0,1:T(8,128)} fusion(f32[128,128]{1,0:T(8,128)S(1)} %fusion.57, f32[8,4,64,256]{3,2,1,0:T(8,128)S(1)} %fusion.14, f32[4,64,8,128]{3,2,1,0:T(8,128)S(1)} %bitcast.136, f32[8,4,64]{2,1,0:T(4,128)S(1)} %add_rsqrt_fusion), kind=kOutput, calls=%fused_computation.27 | convolution fusion | flops 403439616 | bytes 4276224 | tf_op jit(solution)/shard_map/hncd,hnce->hnde/dot_general | solution.py:28
  47.9 28.9 %while.30 = (s32[]{:T(128)}, f32[8,128,128]{2,1,0:T(8,128)}, f32[8,128,128]{2,1,0:T(8,128)}, f32[4,8,128,128]{3,2,1,0:T(8,128)}, f32[4,8,128,128]{3,2,1,0:T(8,12...) while((s32[]{:T(128)}, f32[8,128,128]{2,1,0:T(8,128)}, ...), condition=%wide.region_2.3_spmd.clone, body=%wide.region_1.2_spmd.clone.sunk | while | flops 403046400 | bytes 16254611 | solution.py:110
  51.2 2.5 convolution_add_fusion.7
  53.7 1.4 fusion.107
  58.4 2.5 convolution_add_fusion.7
  60.9 1.4 fusion.107
  65.7 2.5 convolution_add_fusion.7
  68.1 1.4 fusion.107
  72.9 2.5 convolution_add_fusion.7
  75.4 1.4 fusion.107
  80.1 1.9 fusion.43
  82.0 1.9 convolution_subtract_fusion
  84.0 3.1 fusion.18
  87.1 3.1 fusion.22
  90.2 104.3 %all-gather.5.cloned.1.call-done = f32[256,128,128]{2,1,0:T(8,128)} async-done(((f32[8,128,128]{2,1,0:T(8,128)}), f32[256,128,128]{2,1,0:T(8,128)}) %all-gather.5.cloned.1.call-update) | async-done | bytes 16777232 | tf_op jit(solution)/shard_map/all_gather | solution.py:16
  194.5 116.5 %all-gather.7.cloned.1.call-done = f32[256,128,128]{2,1,0:T(8,128)} async-done(((f32[8,128,128]{2,1,0:T(8,128)}), f32[256,128,128]{2,1,0:T(8,128)}) %all-gather.7.cloned.1.call-update) | async-done | bytes 16777232 | tf_op jit(solution)/shard_map/all_gather | solution.py:16
  311.3 2.9 multiply_reduce_fusion
  315.1 8.1 %convolution_bitcast_fusion = f32[4096,1024]{0,1:T(8,128)} fusion(bf16[256,1024]{1,0:T(8,128)(2,1)S(1)} %bitcast.141, bf16[256,4096]{1,0:T(8,128)(2,1)S(1)} %copy-done), kind=kOutput, calls=%fused_computation.18 | convolution fusion | flops 2147483648 | bytes 19398656 | tf_op jit(solution)/shard_map/dot_general | solution.py:124
  323.2 241.2 %reduce-scatter.2.cloned.1.call-done = f32[128,1024]{0,1:T(8,128)} async-done(((f32[4096,1024]{0,1:T(8,128)}), f32[128,1024]{0,1:T(8,128)}) %reduce-scatter.2.cloned.1.call-update) | async-done | bytes 524304 | tf_op jit(solution)/shard_map/reduce_scatter | solution.py:123
  564.4 2.0 copy.37
  (77 shorter events, 32.9 us)
Async XLA Ops:
  7.2 307.9 %copy-start = (bf16[256,4096]{1,0:T(8,128)(2,1)S(1)}, bf16[256,4096]{1,0:T(8,128)(2,1)}, u32[]{:S(2)}) copy-start(bf16[256,4096]{1,0:T(8,128)(2,1)} %param.15) | copy-start | bytes 6291460
  7.2 187.4 %all-gather.5.cloned.1.call-start = ((), (), s32[]{:S(2)}) async-start(), calls=%async_computation.2 | async-start | bytes 17301504 | tf_op jit(solution)/shard_map/all_gather | solution.py:16
  22.1 1.2 copy-start.7
  27.4 5.1 copy-start.2
  47.9 3.3 copy-start.1
  55.1 3.3 copy-start.1
  62.4 3.3 copy-start.1
  69.6 3.3 copy-start.1
  76.8 234.2 %all-gather.7.cloned.1.call-start = ((), (), s32[]{:S(2)}) async-start(), calls=%async_computation.3 | async-start | bytes 17301504 | tf_op jit(solution)/shard_map/all_gather | solution.py:16
  77.6 486.8 %reduce-scatter.2.cloned.1.call-start = ((), (), s32[]{:S(2)}) async-start(), calls=%async_computation.1 | async-start | bytes 17301504 | tf_op jit(solution)/shard_map/reduce_scatter | solution.py:123
  77.6 2.5 copy-start.3
  82.0 1.9 copy-start.6
  83.9 3.1 copy-start.5
  311.3 2.9 copy-start.8
  315.0 8.2 %copy-start.4 = (bf16[32,8,8,128]{3,1,2,0:T(8,128)(2,1)}, bf16[32,8,8,128]{3,1,2,0:T(8,128)(2,1)S(1)}, u32[]{:S(2)}) copy-start(bf16[32,8,8,128]{3,1,2,0:T(8,128)(2,1)S(1)} %copy.68) | copy-start | bytes 1572868
Sparse Core Ops, SparseCore 0:
  76.9 117.5 all-gather.4
  198.0 113.0 all-gather.6
  323.3 241.0 reduce-scatter.1
where the time goes:
time: 579 us; the launch traced here: 573 us
  waiting for transfers between devices  463 us (80%)
  matrix products  73.9 us (13%)
  local copies, waits for them, and re-layouts  15 us (3%)
  between operations  14.3 us (2%)
  other arithmetic  6.92 us (1%)
    reduce_scatter x1, waiting for transfers between devices, on_device(): lax.psum_scatter(lax.dot_general(full_cotangent, attended, (((0,), (0,)),...  241 us
    all_gather x2, waiting for transfers between devices, entering(): gathered = jax.tree.map(lambda a: lax.all_gather(a, axis), part)  221 us
    dot_general x28, matrix products, matmul(): jnp.einsum(pattern, former, latter, precision=highest, preferred_element_...  65.7 us
  transfers between devices with their start and end apart: 3, of which 3 were waited for; matrix products, arithmetic and copies ran while one was open for 2% of the time, Pallas kernels for 0%

commit v1 on v0

v1 whole, which is shorter than its diff:
```python
import functools

import jax
import jax.numpy as jnp
from jax import lax
from jax.experimental import pallas as pl
from jax.experimental.pallas import tpu as pltpu
from jax.sharding import PartitionSpec as P

EPS = 1e-06
CORES = 2
F32 = jnp.float32
BF16 = jnp.bfloat16


def dot(a, b):
    return lax.dot_general(a, b, (((1,), (0,)), ((), ())), preferred_element_type=F32)


def dot_nt(a, b):
    return lax.dot_general(a, b, (((1,), (1,)), ((), ())), preferred_element_type=F32)


def dot_tn(a, b):
    return lax.dot_general(a, b, (((0,), (0,)), ((), ())), preferred_element_type=F32)


def halves(x):
    hi = x.astype(BF16)
    return hi, (x - hi.astype(F32)).astype(BF16)


def mm_packed(a, b):
    n = b.shape[1]
    ah, al = halves(a)
    bh, bl = halves(b)
    left = jnp.concatenate([ah, al], axis=1)
    right = jnp.concatenate(
        [jnp.concatenate([bh, bl], axis=1), jnp.concatenate([bh, jnp.zeros_like(bl)], axis=1)],
        axis=0,
    )
    both = dot(left, right)
    return both[:, :n] + both[:, n:]


def mm3(a, b):
    ah, al = halves(a)
    bh, bl = halves(b)
    return dot(ah, bh) + (dot(ah, bl) + dot(al, bh))


def mm_tall(a, b):
    ah, al = halves(a)
    bh, bl = halves(b)
    left = jnp.concatenate([ah, al], axis=1)
    return dot(left, jnp.concatenate([bh, bh], axis=0)) + dot(ah, bl)


def chunk_inverse(lower, tok, block):
    row = lax.broadcasted_iota(jnp.int32, (block, block), 0)
    col = lax.broadcasted_iota(jnp.int32, (block, block), 1)
    apart = row ^ col
    eye = (row == col).astype(F32)
    diag = []
    for b in range(tok // block):
        part = lower[b * block : (b + 1) * block, b * block : (b + 1) * block]
        inv = eye - jnp.where(apart < 2, part, 0.0)
        diag.append((part, inv))
    size = 2
    while size < block:
        pick = (apart >= size) & (apart < 2 * size)
        diag = [
            (part, inv - mm_packed(mm_packed(inv, jnp.where(pick, part, 0.0)), inv))
            for part, inv in diag
        ]
        size *= 2
    return [inv for _, inv in diag]


def local_head(qb, kb, vb, strength, tok, width):
    block = min(tok, width)
    row = lax.broadcasted_iota(jnp.int32, (tok, tok), 0)
    col = lax.broadcasted_iota(jnp.int32, (tok, tok), 1)
    gram = dot_nt(kb, kb)
    onto = jnp.where(row == col, gram, 0.0)
    r_col = lax.rsqrt(jnp.sum(onto, axis=1, keepdims=True) + EPS)
    r_row = lax.rsqrt(jnp.sum(onto, axis=0, keepdims=True) + EPS)
    lower = jnp.where(row > col, gram * (strength * r_col) * r_row, 0.0)
    invs = chunk_inverse(lower, tok, block)
    kf = kb.astype(F32)
    rhs = jnp.concatenate([kf * (strength * r_col), vb.astype(F32) * strength], axis=1)
    solved = []
    for b in range(tok // block):
        want = rhs[b * block : (b + 1) * block]
        if b > 0:
            want = want - mm3(
                lower[b * block : (b + 1) * block, : b * block], jnp.concatenate(solved, axis=0)
            )
        solved.append(mm_tall(invs[b], want))
    y = jnp.concatenate(solved, axis=0)
    yh, yl = halves(y * r_col)
    kty = dot_tn(kb, yh) + dot_tn(kb, yl)
    frow = lax.broadcasted_iota(jnp.int32, (width, 2 * width), 0)
    fcol = lax.broadcasted_iota(jnp.int32, (width, 2 * width), 1)
    tw = jnp.where(fcol < width, (frow == fcol).astype(F32) - kty, kty)
    scores = jnp.where(row >= col, dot_nt(qb, kb) * r_row, 0.0)
    sy = mm3(scores, y)
    cb = jnp.concatenate([qb.astype(F32) - sy[:, :width], sy[:, width:]], axis=1)
    return tw, cb


def kernel(
    dims,
    q_ref,
    k_ref,
    v_ref,
    beta_ref,
    gain_ref,
    cot_ref,
    att_ref,
    wg_ref,
    cotr,
    cott,
    tw,
    twr,
    cb,
    pre,
    sz,
    snext,
    st_send,
    st,
    attg,
    rs_s,
    rs_r,
    own,
    cot_own_sem,
    cota_s,
    cota_r,
    cotb_s,
    cotb_r,
    tw_s,
    tw_r,
    sz_s,
    sz_r,
    st_s,
    st_r,
    att_s,
    att_r,
    rs_ss,
    rs_rs,
):
    total, planes, group, chips, heads, tok, width, rows, steps = dims
    me = lax.axis_index("ctx")
    z = me // group
    j = me % group
    m = j // CORES
    c = j % CORES
    sib = 1 - c
    cw = CORES * rows
    half = heads * width // CORES
    uw = half // steps

    def remote(src, dst, ssem, rsem, target):
        return pltpu.make_async_remote_copy(
            src_ref=src,
            dst_ref=dst,
            send_sem=ssem,
            recv_sem=rsem,
            device_id={"ctx": target},
            device_id_type=pl.DeviceIdType.MESH,
        )

    barrier = pltpu.get_barrier_semaphore()
    peers = [z * group + (j + k) % group for k in range(1, group)]
    for kz in range(1, planes):
        zz = (z + kz) % planes
        peers += [zz * group + m * CORES + c, zz * group + m * CORES + sib]
    for peer in peers:
        pl.semaphore_signal(
            barrier, inc=1, device_id={"ctx": peer}, device_id_type=pl.DeviceIdType.MESH
        )
    pl.semaphore_wait(barrier, len(peers))

    def cot_cols(zz, mm):
        return cot_ref.at[:, pl.ds(pl.multiple_of((zz * group + mm * CORES) * rows, cw), cw)]

    def cot_a(k, zz):
        mm = (m + k) % chips
        return remote(
            cot_cols(zz, mm),
            cotr.at[j, zz],
            cota_s.at[k, zz],
            cota_r.at[k, zz],
            z * group + mm * CORES + c,
        )

    def cot_mine(zz):
        return pltpu.make_async_copy(cot_cols(zz, m), cotr.at[j, zz], cot_own_sem.at[zz])

    def cot_b(k, zz):
        source = ((m + chips - k) % chips) * CORES + c
        return remote(
            cotr.at[source, zz],
            cotr.at[source, zz],
            cotb_s.at[k, zz],
            cotb_r.at[k, zz],
            z * group + m * CORES + sib,
        )

    for zz in range(planes):
        cot_mine(zz).start()
    for k in range(1, chips):
        for zz in range(planes):
            cot_a(k, zz).start()

    def tw_copy(h, slot):
        return remote(tw.at[h], twr.at[slot], tw_s.at[h], tw_r.at[slot], z * group + h)

    lanes = lax.broadcasted_iota(jnp.int32, (tok, heads), 1)
    batch = 4 if heads % 4 == 0 else 1

    def some_heads(step, _):
        for b in range(batch):
            h = step * batch + b
            cols = pl.ds(pl.multiple_of(h * width, width), width)
            strength = jnp.sum(
                jnp.where(lanes == h, beta_ref[...], 0.0), axis=1, keepdims=True
            )
            got_tw, got_cb = local_head(
                q_ref[:, cols], k_ref[:, cols], v_ref[:, cols], strength, tok, width
            )
            tw[h] = got_tw
            cb[h] = got_cb
        for b in range(batch):
            h = step * batch + b

            @pl.when(h != j)
            def _():
                tw_copy(h, j).start()

        return 0

    lax.fori_loop(0, heads // batch, some_heads, 0)
    twr[j] = tw[j]

    for zz in range(planes):
        cot_mine(zz).wait()
        cot_b(0, zz).start()
    for k in range(1, group):
        tw_copy((j + k) % group, (j + k) % group).wait_recv()

    frow = lax.broadcasted_iota(jnp.int32, (width, 2 * width), 0)
    fcol = lax.broadcasted_iota(jnp.int32, (width, 2 * width), 1)
    pre[0] = (frow == fcol).astype(F32)

    def compose(i, _):
        pair = twr[i]
        pre[i + 1] = mm_tall(pair[:, :width], pre[i]) + jnp.where(fcol < width, 0.0, pair)
        return 0

    lax.fori_loop(0, group, compose, 0)

    def sz_copy(target):
        return remote(snext, sz, sz_s, sz_r, target)

    @pl.when(z == 0)
    def _():
        sz[...] = jnp.zeros_like(sz)

    @pl.when(z > 0)
    def _():
        sz_copy(me).wait_recv()

    state = sz[...]

    @pl.when(z < planes - 1)
    def _():
        pair = pre[group]
        snext[...] = mm_packed(pair[:, :width], state) + pair[:, width:]
        sz_copy(me + group).start()

    def st_copy(i, slot):
        return remote(st_send.at[i], st.at[slot], st_s.at[i], st_r.at[slot], z * group + i)

    for k in range(group):
        i = (j + k) % group
        pair = pre[i]
        st_send[i] = mm_packed(pair[:, :width], state) + pair[:, width:]
        if k > 0:
            st_copy(i, j).start()
    st[j] = st_send[j]

    for k in range(1, chips):
        for zz in range(planes):
            cot_a(k, zz).wait_recv()
            cot_b(k, zz).start()
    for k in range(chips):
        source = ((m + chips - k) % chips) * CORES + c
        at = pl.ds(pl.multiple_of(source * tok, tok), tok)
        for zz in range(planes):
            cott[zz, :, at] = cotr[source, zz].T

    gain = gain_ref[...]

    def att_copy(u, i, ci, slot, sem_s, sem_r):
        return remote(
            att_ref.at[:, pl.ds(pl.multiple_of(ci * half + u * uw, uw), uw)],
            attg.at[u, pl.ds(pl.multiple_of(slot * tok, tok), tok), :],
            att_s.at[u, sem_s],
            att_r.at[u, sem_r],
            z * group + i,
        )

    per = uw // width
    for u in range(steps):
        for ci in range(CORES):
            for e in range(per):
                h = ci * (heads // CORES) + u * per + e

                @pl.when(j != h)
                def _():
                    st_copy(j, h).wait_recv()

                pair = cb[h]
                mixed = pair[:, width:] + mm_packed(pair[:, :width], st[h])
                square = jnp.mean(mixed * mixed, axis=1, keepdims=True)
                att_ref[:, h * width : (h + 1) * width] = (
                    mixed * lax.rsqrt(square + EPS) * gain
                ).astype(BF16)
        for k in range(1, group):
            i = (j + k) % group
            att_copy(u, i, i % CORES, j, i, j).start()
        attg[u, pl.ds(pl.multiple_of(j * tok, tok), tok), :] = att_ref[
            :, pl.ds(pl.multiple_of(c * half + u * uw, uw), uw)
        ]

    for k in range(chips):
        source = ((m + chips - k) % chips) * CORES + sib
        at = pl.ds(pl.multiple_of(source * tok, tok), tok)
        for zz in range(planes):
            remote(
                cotr.at[source, zz],
                cotr.at[source, zz],
                cotb_s.at[k, zz],
                cotb_r.at[k, zz],
                me,
            ).wait_recv()
            cott[zz, :, at] = cotr[source, zz].T

    def rs_copy(u, zz, cc, zs, cs):
        return remote(
            rs_s.at[u, zz, pl.ds(pl.multiple_of(cc * rows, rows), rows), :],
            rs_r.at[u, zs, cs],
            rs_ss.at[u, zz, cc],
            rs_rs.at[u, zs, cs],
            zz * group + m * CORES + cc,
        )

    for u in range(steps):
        for k in range(1, group):
            i = (j + k) % group
            att_copy(u, i, c, i, i, i).wait_recv()
        for kz in list(range(1, planes)) + [0]:
            zz = (z + kz) % planes
            part = dot(cott[zz], attg[u])
            rs_s[u, zz] = part.astype(BF16)
            if kz == 0:
                own[u] = part
                rs_copy(u, zz, sib, z, c).start()
            else:
                rs_copy(u, zz, c, z, c).start()
                rs_copy(u, zz, sib, z, c).start()

    for u in range(steps):
        acc = own[u, pl.ds(pl.multiple_of(c * rows, rows), rows), :]
        for kz in range(1, planes):
            zz = (z + kz) % planes
            rs_copy(u, z, c, zz, c).wait_recv()
            acc = acc + rs_r[u, zz, c].astype(F32)
        wg_ref[:, pl.ds(pl.multiple_of(c * half + u * uw, uw), uw)] = acc
        acc = jnp.zeros((rows, uw), F32)
        for kz in range(planes):
            zz = (z + kz) % planes
            rs_copy(u, z, c, zz, sib).wait_recv()
            acc = acc + rs_r[u, zz, sib].astype(F32)
        wg_ref[:, pl.ds(pl.multiple_of(sib * half + u * uw, uw), uw)] = acc

    for zz in range(planes):
        for k in range(1, chips):
            cot_a(k, zz).wait_send()
        for k in range(chips):
            cot_b(k, zz).wait_send()
    for k in range(1, group):
        i = (j + k) % group
        tw_copy(i, j).wait_send()
        st_copy(i, j).wait_send()
        for u in range(steps):
            att_copy(u, i, i % CORES, j, i, j).wait_send()

    @pl.when(z < planes - 1)
    def _():
        sz_copy(me + group).wait_send()

    for u in range(steps):
        for kz in range(planes):
            zz = (z + kz) % planes
            if kz > 0:
                rs_copy(u, zz, c, z, c).wait_send()
            rs_copy(u, zz, sib, z, c).wait_send()


def on_device(total, joined, query_rows, key_rows, value_rows, beta, norm_gain, out_cotangent):
    tok = query_rows.shape[0]
    heads = beta.shape[1]
    width = query_rows.shape[1] // heads
    if joined > 1:
        out_cotangent = lax.all_gather(out_cotangent, "head", axis=1, tiled=True)
    model = out_cotangent.shape[1]
    rows = model // total
    group = heads
    planes = total // group
    chips = group // CORES
    steps = 2
    half = heads * width // CORES
    uw = half // steps
    dims = (total, planes, group, chips, heads, tok, width, rows, steps)
    vmem = pl.BlockSpec(memory_space=pltpu.VMEM)
    dma = pltpu.SemaphoreType.DMA
    return pl.pallas_call(
        functools.partial(kernel, dims),
        out_shape=(
            jax.ShapeDtypeStruct((tok, heads * width), BF16),
            jax.ShapeDtypeStruct((rows, heads * width), F32),
        ),
        in_specs=[vmem] * 5 + [pl.BlockSpec(memory_space=pl.ANY)],
        out_specs=(vmem, vmem),
        scratch_shapes=[
            pltpu.VMEM((group, planes, tok, CORES * rows), BF16),
            pltpu.VMEM((planes, CORES * rows, group * tok), BF16),
            pltpu.VMEM((heads, width, 2 * width), F32),
            pltpu.VMEM((group, width, 2 * width), F32),
            pltpu.VMEM((heads, tok, 2 * width), F32),
            pltpu.VMEM((group + 1, width, 2 * width), F32),
            pltpu.VMEM((width, width), F32),
            pltpu.VMEM((width, width), F32),
            pltpu.VMEM((group, width, width), F32),
            pltpu.VMEM((heads, width, width), F32),
            pltpu.VMEM((steps, group * tok, uw), BF16),
            pltpu.VMEM((steps, planes, CORES * rows, uw), BF16),
            pltpu.VMEM((steps, planes, CORES, rows, uw), BF16),
            pltpu.VMEM((steps, CORES * rows, uw), F32),
            dma((planes,)),
            dma((chips, planes)),
            dma((chips, planes)),
            dma((chips, planes)),
            dma((chips, planes)),
            dma((heads,)),
            dma((heads,)),
            dma,
            dma,
            dma((group,)),
            dma((heads,)),
            dma((steps, group)),
            dma((steps, group)),
            dma((steps, planes, CORES)),
            dma((steps, planes, CORES)),
        ],
        compiler_params=pltpu.CompilerParams(
            collective_id=0, has_side_effects=True, vmem_limit_bytes=56 * 1024 * 1024
        ),
    )(query_rows, key_rows, value_rows, beta, norm_gain.reshape(1, -1), out_cotangent)


def solution(mesh):
    spec = P("ctx", "head")
    return jax.shard_map(
        functools.partial(on_device, mesh.shape["ctx"], mesh.shape["head"]),
        mesh=mesh,
        in_specs=(spec, spec, spec, spec, P(), spec),
        out_specs=(spec, spec),
        check_vma=False,
    )
```

time: 579 us -> 103 us (0.18)
  waiting for transfers between devices: 463 us -> 0 us
  Pallas kernels: 0 us -> 96.7 us
  matrix products: 73.9 us -> 0 us
  between operations: 14.3 us -> 0.64 us
  local copies, waits for them, and re-layouts: 15 us -> 5.24 us
  other arithmetic: 6.92 us -> 0 us
    reduce_scatter x1 -> x0, waiting for transfers between devices: 241 us -> none  [on_device(): lax.psum_scatter(lax.dot_general(full_cotangent, attended, (((0,), (0,)),...]
    all_gather x2 -> x0, waiting for transfers between devices: 221 us -> none  [entering(): gathered = jax.tree.map(lambda a: lax.all_gather(a, axis), part)]
    pallas_call x0 -> x1, Pallas kernels: none -> 96.7 us  [on_device(): pl.pallas_call(functools.partial(kernel, dims), out_shape=(jax.ShapeDtype...]
    dot_general x29 -> x0, matrix products: 73.9 us -> none  [the longest x28 65.7 us: matmul(): jnp.einsum(pattern, former, latter, precision=highest, preferred_element_...]
    while x16 -> x0, local copies, waits for them, and re-layouts: 8.95 us -> none
  transfers between devices with their start and end apart: 3 -> 0, of which waited for: 3 -> 0; matrix products, arithmetic and copies ran while one was open for 2% -> 0% of each run, Pallas kernels for 0% -> 0%
where the time goes in v1:
time: 103 us
  Pallas kernels  96.7 us (94%)
  local copies, waits for them, and re-layouts  5.24 us (5%)
    pallas_call x1, Pallas kernels, on_device(): pl.pallas_call(functools.partial(kernel, dims), out_shape=(jax.ShapeDtype...  96.7 us
    unnamed x3, local copies, waits for them, and re-layouts  5.24 us

profile of v1, /device:TPU:0, one launch (start us, length us, event | category | flops | bytes accessed | tf_op | source)
XLA Modules:
  0.0 102.6 jit_solution(10736754533344574341)
XLA Ops:
  0.6 1.5 %copy.8.beta_ref = f32[256,8]{1,0:T(8,128)} copy(f32[256,8]{0,1:T(8,128)} %param.9) | data formatting | bytes 16384 | tf_op args[3]
  2.1 96.7 %shard_map.77 = (bf16[256,1024]{1,0:T(8,128)(2,1)}, f32[128,1024]{1,0:T(8,128)}) custom-call(bf16[256,1024]{1,0:T(8,128)(2,1)} %q_ref.1, bf16[256,1024]{1,0:T(8,128)(2,1)} %k_ref.1, bf16[256,1024]{1,0:T(8,128)(2,1)} %v_ref.1, f32[256,8]{1,0:T(8,128)} %copy.8.beta_ref, f32[1,128]{1,0:T(1,128)} %bitcast.1, bf16[256,4096]{1,0:T(8,128)(2,1)} %cot_ref.1), custom_call_target="tpu_custom_call" | custom-call | tf_op jit(solution)/shard_map/pallas_call | solution.py:429
  98.8 1.9 %copy.11 = bf16[256,1024]{1,0:T(8,128)(2,1)} copy(bf16[256,1024]{1,0:T(8,128)(2,1)} %get-tuple-element.4) | data formatting | bytes 1048576
  100.7 1.9 %copy.12 = f32[128,1024]{1,0:T(8,128)} copy(f32[128,1024]{1,0:T(8,128)} %get-tuple-element.5) | data formatting | bytes 1048576

commit v2 on v1

--- a/solution.py
+++ b/solution.py
@@ -120,13 +120,16 @@
     att_ref,
     wg_ref,
     cotr,
-    cott,
+    att_t,
     tw,
     twr,
     cb,
     pre,
+    tree,
+    zp,
     sz,
     snext,
+    scur,
     st_send,
     st,
     attg,
@@ -140,6 +143,8 @@
     cotb_r,
     tw_s,
     tw_r,
+    zp_s,
+    zp_r,
     sz_s,
     sz_r,
     st_s,
@@ -184,24 +189,27 @@
     def cot_cols(zz, mm):
         return cot_ref.at[:, pl.ds(pl.multiple_of((zz * group + mm * CORES) * rows, cw), cw)]
 
+    def came(source, zz):
+        return cotr.at[zz, pl.ds(pl.multiple_of(source * tok, tok), tok), :]
+
     def cot_a(k, zz):
         mm = (m + k) % chips
         return remote(
             cot_cols(zz, mm),
-            cotr.at[j, zz],
+            came(j, zz),
             cota_s.at[k, zz],
             cota_r.at[k, zz],
             z * group + mm * CORES + c,
         )
 
     def cot_mine(zz):
-        return pltpu.make_async_copy(cot_cols(zz, m), cotr.at[j, zz], cot_own_sem.at[zz])
+        return pltpu.make_async_copy(cot_cols(zz, m), came(j, zz), cot_own_sem.at[zz])
 
     def cot_b(k, zz):
         source = ((m + chips - k) % chips) * CORES + c
         return remote(
-            cotr.at[source, zz],
-            cotr.at[source, zz],
+            came(source, zz),
+            came(source, zz),
             cotb_s.at[k, zz],
             cotb_r.at[k, zz],
             z * group + m * CORES + sib,
@@ -216,7 +224,9 @@
     def tw_copy(h, slot):
         return remote(tw.at[h], twr.at[slot], tw_s.at[h], tw_r.at[slot], z * group + h)
 
-    lanes = lax.broadcasted_iota(jnp.int32, (tok, heads), 1)
+    turn = lax.broadcasted_iota(jnp.int32, (tok, tok), 0) == lax.broadcasted_iota(
+        jnp.int32, (tok, tok), 1
+    )
     batch = 4 if heads % 4 == 0 else 1
 
     def some_heads(step, _):
@@ -224,7 +234,7 @@
             h = step * batch + b
             cols = pl.ds(pl.multiple_of(h * width, width), width)
             strength = jnp.sum(
-                jnp.where(lanes == h, beta_ref[...], 0.0), axis=1, keepdims=True
+                jnp.where(turn, beta_ref[pl.ds(h, 1), :], 0.0), axis=1, keepdims=True
             )
             got_tw, got_cb = local_head(
                 q_ref[:, cols], k_ref[:, cols], v_ref[:, cols], strength, tok, width
@@ -243,69 +253,111 @@
     lax.fori_loop(0, heads // batch, some_heads, 0)
     twr[j] = tw[j]
 
-    for zz in range(planes):
-        cot_mine(zz).wait()
-        cot_b(0, zz).start()
     for k in range(1, group):
         tw_copy((j + k) % group, (j + k) % group).wait_recv()
 
     frow = lax.broadcasted_iota(jnp.int32, (width, 2 * width), 0)
     fcol = lax.broadcasted_iota(jnp.int32, (width, 2 * width), 1)
+
+    def compose(later, earlier):
+        return mm_tall(later[:, :width], earlier) + jnp.where(fcol < width, 0.0, later)
+
+    levels = [[twr.at[i] for i in range(group)]]
+    used = 0
+    while len(levels[-1]) > 1:
+        below = levels[-1]
+        above = [tree.at[used + i] for i in range(len(below) // 2)]
+        for i, node in enumerate(above):
+            node[...] = compose(below[2 * i + 1][...], below[2 * i][...])
+        used += len(above)
+        levels.append(above)
+    top = tree.at[used - 1]
+
+    def zp_copy(target):
+        return remote(top, zp, zp_s, zp_r, target)
+
+    def sz_copy(n, target):
+        return remote(snext, sz, sz_s.at[n], sz_r, target)
+
+    @pl.when((z % 2 == 0) & (z < planes - 1))
+    def _():
+        zp_copy(me + group).start()
+
+    def odd_state():
+        zp_copy(me).wait_recv()
+
+        @pl.when(z == 1)
+        def _():
+            scur[...] = zp[:, width:]
+
+        @pl.when(z > 1)
+        def _():
+            sz_copy(0, me).wait_recv()
+            scur[...] = mm_packed(zp[:, :width], sz[...]) + zp[:, width:]
+
+    @pl.when((z % 2 == 1) & (z < planes - 1))
+    def _():
+        odd_state()
+        snext[...] = mm_packed(top[:, :width], scur[...]) + top[:, width:]
+        sz_copy(0, me + group).start()
+
+        @pl.when(z < planes - 2)
+        def _():
+            sz_copy(1, me + 2 * group).start()
+
     pre[0] = (frow == fcol).astype(F32)
-
-    def compose(i, _):
-        pair = twr[i]
-        pre[i + 1] = mm_tall(pair[:, :width], pre[i]) + jnp.where(fcol < width, 0.0, pair)
-        return 0
-
-    lax.fori_loop(0, group, compose, 0)
-
-    def sz_copy(target):
-        return remote(snext, sz, sz_s, sz_r, target)
+    span = group // 2
+    depth = len(levels) - 2
+    while span >= 1:
+        for i in range(0, group, 2 * span):
+            node = levels[depth][i // span]
+            if i == 0:
+                pre[span] = node[...]
+            else:
+                pre[i + span] = compose(node[...], pre[i])
+        span //= 2
+        depth -= 1
+
+    @pl.when((z % 2 == 1) & (z == planes - 1))
+    def _():
+        odd_state()
+
+    @pl.when((z % 2 == 0) & (z > 0))
+    def _():
+        sz_copy(0, me).wait_recv()
+        scur[...] = sz[...]
 
     @pl.when(z == 0)
     def _():
-        sz[...] = jnp.zeros_like(sz)
-
-    @pl.when(z > 0)
-    def _():
-        sz_copy(me).wait_recv()
-
-    state = sz[...]
-
-    @pl.when(z < planes - 1)
-    def _():
-        pair = pre[group]
-        snext[...] = mm_packed(pair[:, :width], state) + pair[:, width:]
-        sz_copy(me + group).start()
+        scur[...] = jnp.zeros_like(scur)
+
+    state = scur[...]
 
     def st_copy(i, slot):
         return remote(st_send.at[i], st.at[slot], st_s.at[i], st_r.at[slot], z * group + i)
 
-    for k in range(group):
+    for k in range(1, group + 1):
         i = (j + k) % group
         pair = pre[i]
         st_send[i] = mm_packed(pair[:, :width], state) + pair[:, width:]
-        if k > 0:
+        if k < group:
             st_copy(i, j).start()
     st[j] = st_send[j]
 
-    for k in range(1, chips):
+    for k in range(chips):
         for zz in range(planes):
-            cot_a(k, zz).wait_recv()
+            if k == 0:
+                cot_mine(zz).wait()
+            else:
+                cot_a(k, zz).wait_recv()
             cot_b(k, zz).start()
-    for k in range(chips):
-        source = ((m + chips - k) % chips) * CORES + c
-        at = pl.ds(pl.multiple_of(source * tok, tok), tok)
-        for zz in range(planes):
-            cott[zz, :, at] = cotr[source, zz].T
 
     gain = gain_ref[...]
 
     def att_copy(u, i, ci, slot, sem_s, sem_r):
         return remote(
-            att_ref.at[:, pl.ds(pl.multiple_of(ci * half + u * uw, uw), uw)],
-            attg.at[u, pl.ds(pl.multiple_of(slot * tok, tok), tok), :],
+            att_t.at[u, ci],
+            attg.at[u, :, pl.ds(pl.multiple_of(slot * tok, tok), tok)],
             att_s.at[u, sem_s],
             att_r.at[u, sem_r],
             z * group + i,
@@ -324,32 +376,28 @@
                 pair = cb[h]
                 mixed = pair[:, width:] + mm_packed(pair[:, :width], st[h])
                 square = jnp.mean(mixed * mixed, axis=1, keepdims=True)
-                att_ref[:, h * width : (h + 1) * width] = (
-                    mixed * lax.rsqrt(square + EPS) * gain
-                ).astype(BF16)
+                normed = mixed * lax.rsqrt(square + EPS) * gain
+                att_ref[:, h * width : (h + 1) * width] = normed.astype(BF16)
+                att_t[u, ci, e * width : (e + 1) * width, :] = normed.T.astype(BF16)
         for k in range(1, group):
             i = (j + k) % group
             att_copy(u, i, i % CORES, j, i, j).start()
-        attg[u, pl.ds(pl.multiple_of(j * tok, tok), tok), :] = att_ref[
-            :, pl.ds(pl.multiple_of(c * half + u * uw, uw), uw)
-        ]
+        attg[u, :, pl.ds(pl.multiple_of(j * tok, tok), tok)] = att_t[u, c]
 
     for k in range(chips):
         source = ((m + chips - k) % chips) * CORES + sib
-        at = pl.ds(pl.multiple_of(source * tok, tok), tok)
         for zz in range(planes):
             remote(
-                cotr.at[source, zz],
-                cotr.at[source, zz],
+                came(source, zz),
+                came(source, zz),
                 cotb_s.at[k, zz],
                 cotb_r.at[k, zz],
                 me,
             ).wait_recv()
-            cott[zz, :, at] = cotr[source, zz].T
 
     def rs_copy(u, zz, cc, zs, cs):
         return remote(
-            rs_s.at[u, zz, pl.ds(pl.multiple_of(cc * rows, rows), rows), :],
+            rs_s.at[u, zz, :, pl.ds(pl.multiple_of(cc * rows, rows), rows)],
             rs_r.at[u, zs, cs],
             rs_ss.at[u, zz, cc],
             rs_rs.at[u, zs, cs],
@@ -362,7 +410,7 @@
             att_copy(u, i, c, i, i, i).wait_recv()
         for kz in list(range(1, planes)) + [0]:
             zz = (z + kz) % planes
-            part = dot(cott[zz], attg[u])
+            part = dot(attg[u], cotr[zz])
             rs_s[u, zz] = part.astype(BF16)
             if kz == 0:
                 own[u] = part
@@ -372,18 +420,18 @@
                 rs_copy(u, zz, sib, z, c).start()
 
     for u in range(steps):
-        acc = own[u, pl.ds(pl.multiple_of(c * rows, rows), rows), :]
+        acc = own[u, :, pl.ds(pl.multiple_of(c * rows, rows), rows)]
         for kz in range(1, planes):
             zz = (z + kz) % planes
             rs_copy(u, z, c, zz, c).wait_recv()
             acc = acc + rs_r[u, zz, c].astype(F32)
-        wg_ref[:, pl.ds(pl.multiple_of(c * half + u * uw, uw), uw)] = acc
-        acc = jnp.zeros((rows, uw), F32)
+        wg_ref[:, pl.ds(pl.multiple_of(c * half + u * uw, uw), uw)] = acc.T
+        acc = jnp.zeros((uw, rows), F32)
         for kz in range(planes):
             zz = (z + kz) % planes
             rs_copy(u, z, c, zz, sib).wait_recv()
             acc = acc + rs_r[u, zz, sib].astype(F32)
-        wg_ref[:, pl.ds(pl.multiple_of(sib * half + u * uw, uw), uw)] = acc
+        wg_ref[:, pl.ds(pl.multiple_of(sib * half + u * uw, uw), uw)] = acc.T
 
     for zz in range(planes):
         for k in range(1, chips):
@@ -397,9 +445,17 @@
         for u in range(steps):
             att_copy(u, i, i % CORES, j, i, j).wait_send()
 
-    @pl.when(z < planes - 1)
-    def _():
-        sz_copy(me + group).wait_send()
+    @pl.when((z % 2 == 0) & (z < planes - 1))
+    def _():
+        zp_copy(me + group).wait_send()
+
+    @pl.when((z % 2 == 1) & (z < planes - 1))
+    def _():
+        sz_copy(0, me + group).wait_send()
+
+        @pl.when(z < planes - 2)
+        def _():
+            sz_copy(1, me + 2 * group).wait_send()
 
     for u in range(steps):
         for kz in range(planes):
@@ -407,6 +463,11 @@
             if kz > 0:
                 rs_copy(u, zz, c, z, c).wait_send()
             rs_copy(u, zz, sib, z, c).wait_send()
+
+
+def hand_over(att_in, wg_in, att_out, wg_out):
+    att_out[...] = att_in[...]
+    wg_out[...] = wg_in[...]
 
 
 def on_device(total, joined, query_rows, key_rows, value_rows, beta, norm_gain, out_cotangent):
@@ -420,13 +481,13 @@
     group = heads
     planes = total // group
     chips = group // CORES
-    steps = 2
+    steps = 4
     half = heads * width // CORES
     uw = half // steps
     dims = (total, planes, group, chips, heads, tok, width, rows, steps)
     vmem = pl.BlockSpec(memory_space=pltpu.VMEM)
     dma = pltpu.SemaphoreType.DMA
-    return pl.pallas_call(
+    attended, weight_grad = pl.pallas_call(
         functools.partial(kernel, dims),
         out_shape=(
             jax.ShapeDtypeStruct((tok, heads * width), BF16),
@@ -435,20 +496,23 @@
         in_specs=[vmem] * 5 + [pl.BlockSpec(memory_space=pl.ANY)],
         out_specs=(vmem, vmem),
         scratch_shapes=[
-            pltpu.VMEM((group, planes, tok, CORES * rows), BF16),
-            pltpu.VMEM((planes, CORES * rows, group * tok), BF16),
+            pltpu.VMEM((planes, group * tok, CORES * rows), BF16),
+            pltpu.VMEM((steps, CORES, uw, tok), BF16),
             pltpu.VMEM((heads, width, 2 * width), F32),
             pltpu.VMEM((group, width, 2 * width), F32),
             pltpu.VMEM((heads, tok, 2 * width), F32),
-            pltpu.VMEM((group + 1, width, 2 * width), F32),
+            pltpu.VMEM((group, width, 2 * width), F32),
+            pltpu.VMEM((group - 1, width, 2 * width), F32),
+            pltpu.VMEM((width, 2 * width), F32),
+            pltpu.VMEM((width, width), F32),
             pltpu.VMEM((width, width), F32),
             pltpu.VMEM((width, width), F32),
             pltpu.VMEM((group, width, width), F32),
             pltpu.VMEM((heads, width, width), F32),
-            pltpu.VMEM((steps, group * tok, uw), BF16),
-            pltpu.VMEM((steps, planes, CORES * rows, uw), BF16),
-            pltpu.VMEM((steps, planes, CORES, rows, uw), BF16),
-            pltpu.VMEM((steps, CORES * rows, uw), F32),
+            pltpu.VMEM((steps, uw, group * tok), BF16),
+            pltpu.VMEM((steps, planes, uw, CORES * rows), BF16),
+            pltpu.VMEM((steps, planes, CORES, uw, rows), BF16),
+            pltpu.VMEM((steps, uw, CORES * rows), F32),
             dma((planes,)),
             dma((chips, planes)),
             dma((chips, planes)),
@@ -457,6 +521,8 @@
             dma((heads,)),
             dma((heads,)),
             dma,
+            dma,
+            dma((2,)),
             dma,
             dma((group,)),
             dma((heads,)),
@@ -468,7 +534,16 @@
         compiler_params=pltpu.CompilerParams(
             collective_id=0, has_side_effects=True, vmem_limit_bytes=56 * 1024 * 1024
         ),
-    )(query_rows, key_rows, value_rows, beta, norm_gain.reshape(1, -1), out_cotangent)
+    )(query_rows, key_rows, value_rows, beta.T, norm_gain.reshape(1, -1), out_cotangent)
+    return pl.pallas_call(
+        hand_over,
+        out_shape=(
+            jax.ShapeDtypeStruct(attended.shape, BF16),
+            jax.ShapeDtypeStruct(weight_grad.shape, F32),
+        ),
+        in_specs=[vmem] * 2,
+        out_specs=(vmem, vmem),
+    )(attended, weight_grad)
 
 
 def solution(mesh):

time: 103 us -> 95.7 us (0.929)
  local copies, waits for them, and re-layouts: 5.24 us -> 0 us
  Pallas kernels: 96.7 us -> 94.9 us
    unnamed x3 -> x0, local copies, waits for them, and re-layouts: 5.24 us -> none
    pallas_call x1, Pallas kernels: 96.7 us -> 92.7 us  [on_device(): pl.pallas_call(functools.partial(kernel, dims), out_shape=(jax.ShapeDtype...]
    pallas_call x0 -> x1, Pallas kernels: none -> 2.2 us  [on_device(): pl.pallas_call(hand_over, out_shape=(jax.ShapeDtypeStruct(attended.shape,...]
where the time goes in v2:
time: 95.7 us; the launch traced here: 95.5 us
  Pallas kernels  94.9 us (99%)
    pallas_call x1, Pallas kernels, on_device(): pl.pallas_call(functools.partial(kernel, dims), out_shape=(jax.ShapeDtype...  92.7 us
    pallas_call x1, Pallas kernels, on_device(): pl.pallas_call(hand_over, out_shape=(jax.ShapeDtypeStruct(attended.shape,...  2.2 us

profile of v2, /device:TPU:0, one launch (start us, length us, event | category | flops | bytes accessed | tf_op | source)
XLA Modules:
  0.0 95.5 jit_solution(9630283765480360364)
XLA Ops:
  0.6 92.7 %shard_map.77 = (bf16[256,1024]{1,0:T(8,128)(2,1)}, f32[128,1024]{1,0:T(8,128)}) custom-call(bf16[256,1024]{1,0:T(8,128)(2,1)} %q_ref.1, bf16[256,1024]{1,0:T(8,128)(2,1)} %k_ref.1, bf16[256,1024]{1,0:T(8,128)(2,1)} %v_ref.1, f32[8,256]{1,0:T(8,128)} %bitcast.2, f32[1,128]{1,0:T(1,128)} %bitcast.3, bf16[256,4096]{1,0:T(8,128)(2,1)} %cot_ref.1), custom_call_target="tpu_custom_call" | custom-call | tf_op jit(solution)/shard_map/pallas_call | solution.py:490
  93.3 2.2 %shard_map.78 = (bf16[256,1024]{1,0:T(8,128)(2,1)}, f32[128,1024]{1,0:T(8,128)}) custom-call(bf16[256,1024]{1,0:T(8,128)(2,1)} %get-tuple-element.4.att_in, f32[128,1024]{1,0:T(8,128)} %get-tuple-element.5.wg_in), custom_call_target="tpu_custom_call" | custom-call | tf_op jit(solution)/shard_map/pallas_call | solution.py:538
